TPU v7x, 32 devices: a whole 2x2x4 slice. The times are simulated.
32 devices in a mesh: groups: 2 (over y), replica: 4 (over x, core), tensor: 4 (over z).
Axes of the slice: x: 2, y: 2, z: 4, core: 2. Of those that a mesh axis runs over, the one named last changes fastest.
Arguments:
- tokens: bfloat16 [8, 768, 4096], P(('groups', 'replica'), None, 'tensor'), parts along dimension 0, may hold values from -16 to 16
- lengths: int32 [8], P(('groups', 'replica')), parts along dimension 0, may hold values from 1 to 768, 1536 in all
- block_adapter_index: int32 [8], P(('groups', 'replica')), parts along dimension 0, may hold values from 0 to 7
- cache_page_index: int32 [8, 12], P(('groups', 'replica')), parts along dimension 0, may hold values from 0 to 11, each once within a row
- query_matrix: bfloat16 [4096, 2048], P(None, 'tensor'), may hold values from -0.09375 to 0.09375
- key_matrix: bfloat16 [4096, 512], P(None, 'tensor'), may hold values from -0.09375 to 0.09375
- value_matrix: bfloat16 [4096, 512], P(None, 'tensor'), may hold values from -0.09375 to 0.09375
- down_factors: bfloat16 [8, 4096, 128], P('replica', 'tensor'), may hold values from -0.09375 to 0.09375
- query_up_factors: bfloat16 [8, 64, 2048], P('replica', None, 'tensor'), may hold values from -0.75 to 0.75
- value_up_factors: bfloat16 [8, 64, 512], P('replica', None, 'tensor'), may hold values from -0.75 to 0.75
Outputs:
- attended: bfloat16 [8, 768, 2048], P(('groups', 'replica'), None, 'tensor'), parts along dimension 0
- kv_pages: bfloat16 [8, 12, 2, 64, 512], P(('groups', 'replica'), None, None, None, 'tensor'), parts along dimension 0
There are 2 independent parts, one for each index of `groups`. A program takes and returns all parts, laid end to end along the dimension named above; an argument that names none is the same for every part. Nothing has to cross between parts.
Inputs may be any that keep to these rules, and one draw needn't show every extreme that they name: The lengths of one part sum to 1536, and some block is 768 long. `cache_page_index`: each row is a permutation of the block's pages.
All inputs are finite; a program needn't handle non-finite values.
Results may differ from a plain program's by a relative error of at most 0.008.
The roundings to bfloat16 on the way count: a program that leaves them out, or rounds other values in their place, can miss the bound.
Values may be sent and summed in bfloat16 or wider, within the bound.
A program may use at most 64 MiB of HBM per device.

v0:
```python
import jax
import jax.numpy as jnp
from jax import lax
from jax.sharding import PartitionSpec as P

HEAD_SIZE = 128
PAGE = 64


def rope_tables(length, width):
    half_width = width // 2
    exponent = 2.0 * jnp.arange(half_width, dtype=jnp.float32) / width
    frequency = jnp.exp(-jnp.log(500000.0) * exponent)
    angles = jnp.arange(length, dtype=jnp.float32)[:, None] * frequency[None, :]
    return (jnp.cos(angles), jnp.sin(angles))


def rotate(values, cosine, sine):
    half_width = values.shape[-1] // 2
    first = values[..., :half_width]
    second = values[..., half_width:]
    cos_rows = cosine[:, None, :]
    sin_rows = sine[:, None, :]
    return jnp.concatenate(
        [first * cos_rows - second * sin_rows, second * cos_rows + first * sin_rows], axis=-1
    )


def body(
    tokens,
    lengths,
    block_adapter_index,
    cache_page_index,
    query_matrix,
    key_matrix,
    value_matrix,
    down_factors,
    query_up_factors,
    value_up_factors,
):
    row_count = tokens.shape[1]
    query_width = query_matrix.shape[1]
    kv_width = key_matrix.shape[1]
    rank_total = query_up_factors.shape[1]
    own_rows = tokens[0]
    own_length = lengths[0]
    own_adapter = block_adapter_index[0]
    start_sets = (
        jnp.zeros(down_factors.shape[1:], jnp.bfloat16),
        jnp.zeros(query_up_factors.shape[1:], jnp.bfloat16),
        jnp.zeros(value_up_factors.shape[1:], jnp.bfloat16),
    )
    pieces = (
        lax.all_gather(down_factors, "replica", axis=0, tiled=True),
        lax.all_gather(query_up_factors, "replica", axis=0, tiled=True),
        lax.all_gather(value_up_factors, "replica", axis=0, tiled=True),
    )
    hits = jnp.arange(pieces[0].shape[0], dtype=jnp.int32) == own_adapter
    picked = []
    for held, piece in zip(start_sets, pieces):
        mask = hits.reshape((-1,) + (1,) * (piece.ndim - 1))
        picked.append(jnp.sum(jnp.where(mask, piece, jnp.zeros_like(piece)), axis=0))
    down_own, up_query_own, up_value_own = tuple(picked)
    partial_down = jnp.dot(own_rows, down_own, preferred_element_type=jnp.float32)
    down_projected = lax.psum(partial_down, "tensor").astype(jnp.bfloat16)
    positions = jnp.arange(row_count, dtype=jnp.int32)
    live = positions < own_length
    piece = lax.all_gather(own_rows, "tensor", axis=1, tiled=True)
    q_part = jnp.dot(piece, query_matrix, preferred_element_type=jnp.float32)
    k_part = jnp.dot(piece, key_matrix, preferred_element_type=jnp.float32)
    v_part = jnp.dot(piece, value_matrix, preferred_element_type=jnp.float32)
    query_adapted = q_part + jnp.dot(
        down_projected[:, :rank_total], up_query_own, preferred_element_type=jnp.float32
    )
    value_adapted = v_part + jnp.dot(
        down_projected[:, rank_total:], up_value_own, preferred_element_type=jnp.float32
    )
    q_heads = query_width // HEAD_SIZE
    kv_heads = kv_width // HEAD_SIZE
    group_size = q_heads // kv_heads
    cosine, sine = rope_tables(row_count, HEAD_SIZE)
    q_rot = rotate(query_adapted.reshape(row_count, q_heads, HEAD_SIZE), cosine, sine)
    k_rot = rotate(k_part.reshape(row_count, kv_heads, HEAD_SIZE), cosine, sine)
    query = q_rot.astype(jnp.bfloat16)
    key_rows = jnp.where(live[:, None, None], k_rot, 0.0).astype(jnp.bfloat16)
    value_rows = (
        jnp.where(live[:, None], value_adapted, 0.0)
        .astype(jnp.bfloat16)
        .reshape(row_count, kv_heads, HEAD_SIZE)
    )
    grouped = query.reshape(row_count, kv_heads, group_size, HEAD_SIZE)
    scores = jnp.einsum(
        "tkgd,skd->kgts", grouped, key_rows, preferred_element_type=jnp.float32
    ) * HEAD_SIZE ** (-0.5)
    causal = positions[None, :] <= positions[:, None]
    scores = jnp.where(causal, scores, -jnp.inf)
    peak = jnp.max(scores, axis=-1, keepdims=True)
    weights = jnp.exp(scores - peak)
    probs = (weights / jnp.sum(weights, axis=-1, keepdims=True)).astype(jnp.bfloat16)
    mixed = jnp.einsum("kgts,skd->tkgd", probs, value_rows, preferred_element_type=jnp.float32)
    attended = jnp.where(live[:, None], mixed.reshape(row_count, q_heads * HEAD_SIZE), 0.0).astype(
        jnp.bfloat16
    )
    keys_paged = key_rows.reshape(row_count // PAGE, PAGE, kv_width)
    values_paged = value_rows.reshape(row_count // PAGE, PAGE, kv_width)
    stacked = jnp.stack([keys_paged, values_paged], axis=1)
    pages = jnp.zeros_like(stacked).at[cache_page_index[0]].set(stacked)
    return (attended[None], pages[None])


def solution(mesh):
    in_specs = (
        P(("groups", "replica"), None, "tensor"),
        P(("groups", "replica")),
        P(("groups", "replica")),
        P(("groups", "replica"), None),
        P(None, "tensor"),
        P(None, "tensor"),
        P(None, "tensor"),
        P("replica", "tensor", None),
        P("replica", None, "tensor"),
        P("replica", None, "tensor"),
    )
    out_specs = (
        P(("groups", "replica"), None, "tensor"),
        P(("groups", "replica"), None, None, None, "tensor"),
    )
    return jax.shard_map(body, mesh=mesh, in_specs=in_specs, out_specs=out_specs, check_vma=False)
```

profile of v0, /device:TPU:0, one launch (start us, length us, event | category | flops | bytes accessed | tf_op | source)
XLA Modules:
  0.0 208.8 jit_solution(12812042348711353008)
XLA Ops:
  7.2 0.7 all-gather.4.cloned.1.call-update
  8.0 0.7 all-gather.6.cloned.1.call-update
  10.0 6.7 %all_gather.14 = bf16[8,64,128]{2,1,0:T(8,128)(2,1)S(1)} all-gather(bf16[2,64,128]{2,1,0:T(8,128)(2,1)} %param.19), channel_id=1, replica_groups=mesh['groups'=2,'replica'=4,'tensor'=4] {'replica'}, dimensions={0}, use_global_device_ids=true | all-gather | bytes 163840 | tf_op jit(solution)/shard_map/all_gather | solution.py:56
  16.8 0.2 iota_compare_fusion
  17.0 10.0 %all_gather.15 = bf16[8,64,512]{2,1,0:T(8,128)(2,1)S(1)} all-gather(bf16[2,64,512]{2,1,0:T(8,128)(2,1)} %param.18), channel_id=1, replica_groups=mesh['groups'=2,'replica'=4,'tensor'=4] {'replica'}, dimensions={0}, use_global_device_ids=true | all-gather | bytes 655360 | tf_op jit(solution)/shard_map/all_gather | solution.py:55
  27.0 0.1 select_reduce_fusion.1
  27.1 2.3 %fusion.27 = (f32[768,64]{1,0:T(8,128)}, f32[768,64]{1,0:T(8,128)}) fusion(f32[64]{0:T(128)S(1)} %multiply_exponential_fusion), kind=kLoop, calls=%fused_computation.39 | loop fusion | flops 49152 | bytes 393472 | tf_op jit(solution)/shard_map/cos | solution.py:15
  29.4 7.3 %all-gather.4.cloned.1.call-done = bf16[8,1024,128]{2,1,0:T(8,128)(2,1)} async-done(((bf16[2,1024,128]{2,1,0:T(8,128)(2,1)}), bf16[8,1024,128]{2,1,0:T(8,128)(2,1)}) %all-gather.4.cloned.1.call-update) | async-done | bytes 2097168 | tf_op jit(solution)/shard_map/all_gather | solution.py:54
  36.7 2.1 select_reduce_fusion
  38.8 1.4 fusion.12
  40.2 39.7 %all-reduce.1 = bf16[768,128]{0,1:T(8,128)(2,1)} all-reduce(f32[768,128]{0,1:T(8,128)} %fusion.12), channel_id=1, replica_groups=mesh['groups'=2,'replica'=4,'tensor'=4] {'tensor'}, use_global_device_ids=true, to_apply=%region_1.2 | all-reduce | flops 98304 | bytes 589824 | tf_op jit(solution)/shard_map/psum | solution.py:65
  79.9 83.2 %all-gather.6.cloned.1.call-done = bf16[1,768,4096]{2,1,0:T(8,128)(2,1)} async-done(((bf16[1,768,1024]{2,1,0:T(8,128)(2,1)}), bf16[1,768,4096]{2,1,0:T(8,128)(2,1)}) %all-gather.6.cloned.1.call-update) | async-done | bytes 6291472 | tf_op jit(solution)/shard_map/all_gather | solution.py:68
  163.0 4.7 %fusion.15 = f32[768,1,128]{2,0,1:T(8,128)S(1)} fusion(bf16[4096,128]{1,0:T(8,128)(2,1)S(1)} %copy-done, bf16[1,768,4096]{2,1,0:T(8,128)(2,1)} %all-gather.6.cloned.1.call-done), kind=kOutput, calls=%fused_computation.23 | convolution fusion | flops 805306368 | bytes 7733248 | tf_op jit(solution)/shard_map/dot_general | solution.py:70
  167.7 2.4 %multiply_subtract_fusion = (bf16[768,1,64]{2,0,1:T(8,128)(2,1)S(1)}, bf16[768,1,64]{2,0,1:T(8,128)(2,1)}) fusion(f32[768,1,128]{2,0,1:T(8,128)S(1)} %fusion.15, f32[64]{0:T(128)S(1)} %multiply_exponential_fusion), kind=kLoop, calls=%fused_computation.41 | loop fusion | flops 442368 | bytes 590080 | tf_op jit(solution)/shard_map/sub | solution.py:25
  170.1 5.7 %fusion.2 = f32[768,512]{0,1:T(8,128)S(1)} fusion(bf16[4096,512]{1,0:T(8,128)(2,1)} %param.14, bf16[1,768,4096]{2,1,0:T(8,128)(2,1)S(1)} %copy-done.11), kind=kOutput, calls=%fused_computation.6 | convolution fusion | flops 3221225472 | bytes 12058624 | tf_op jit(solution)/shard_map/dot_general | solution.py:69
  175.8 0.4 convolution_add_fusion
  176.2 1.3 fusion.43
  177.6 1.6 copy.35
  179.2 2.8 %copy.34 = f32[768,4,64]{2,0,1:T(8,128)} copy(f32[768,4,64]{0,2,1:T(8,128)} %get-tuple-element.5) | data formatting | bytes 1572864
  181.9 5.0 %fusion.6 = f32[768,128]{1,0:T(8,128)S(1)} fusion(bf16[4096,128]{1,0:T(8,128)(2,1)} %param.16, bf16[1,768,4096]{2,1,0:T(8,128)(2,1)} %all-gather.6.cloned.1.call-done), kind=kOutput, calls=%fused_computation.10 | convolution fusion | flops 805306368 | bytes 7733248 | tf_op jit(solution)/shard_map/dot_general | solution.py:71
  186.9 0.2 fusion.19
  187.2 0.4 subtract_convert_fusion
  187.6 0.2 copy-done.3
  187.8 2.3 %fusion.1 = (f32[4,768]{1,0:T(4,128)S(1)}, f32[768,768,4]{1,0,2:T(8,128)S(1)}) fusion(pred[768,768]{0,1:T(8,128)(4,1)S(1)} %iota_compare_fusion, bf16[768,4,64]{2,0,1:T(8,128)(2,1)S(1)} %get-tuple-element.3, bf16[768,4,64]{2,0,1:T(8,128)(2,1)S(1)} %get-tuple-element.2, bf16[768,64]{1,0:T(8,128)(2,1)S(1)} %bitcast.79, bf16[768,64]{1,0:T(8,128)(2,1)S(1)} %bitcast.77, ...), kind=kOutput, calls=%fused_computation.5 | convolution fusion | flops 613118976 | bytes 11023104 | tf_op jit(solution)/shard_map/tkgd,skd->kgts/dot_general | solution.py:92
  190.2 2.0 fusion
  192.2 4.1 %fusion.8 = bf16[128,4,768]{2,0,1:T(8,128)(2,1)} fusion(f32[768,768,4]{1,0,2:T(8,128)S(1)} %get-tuple-element.11, f32[4,768]{1,0:T(4,128)S(1)} %fusion, f32[4,768]{1,0:T(4,128)S(1)} %get-tuple-element.10, pred[768,768]{0,1:T(8,128)(4,1)S(1)} %iota_compare_fusion, bf16[768,128]{1,0:T(8,128)(2,1)S(1)} %fusion.19), kind=kOutput, calls=%fused_computation.12 | convolution fusion | flops 615776256 | bytes 11034624 | tf_op jit(solution)/shard_map/kgts,skd->tkgd/dot_general | solution.py:100
  196.3 1.4 copy.26
  197.7 1.1 select_convert_fusion
  198.9 0.2 fusion.25
  199.1 1.0 pad_maximum_fusion
  200.2 1.0 scatter_fusion
  201.2 0.7 copy-done.5
  (33 shorter events, 0.3 us)
Async XLA Ops:
  7.2 155.8 %copy-start = (bf16[4096,128]{1,0:T(8,128)(2,1)S(1)}, bf16[4096,128]{1,0:T(8,128)(2,1)}, u32[]{:S(2)}) copy-start(bf16[4096,128]{1,0:T(8,128)(2,1)} %param.15) | copy-start | bytes 3145732
  7.2 31.6 %copy-start.1 = (bf16[1,768,1024]{2,1,0:T(8,128)(2,1)S(1)}, bf16[1,768,1024]{2,1,0:T(8,128)(2,1)}, u32[]{:S(2)}) copy-start(bf16[1,768,1024]{2,1,0:T(8,128)(2,1)} %param.10) | copy-start | bytes 4718596
  7.2 19.9 %copy-start.12 = (s32[1,12]{1,0:T(1,128)S(1)}, s32[1,12]{1,0:T(1,128)}, u32[]{:S(2)}) copy-start(s32[1,12]{1,0:T(1,128)} %param.13) | copy-start | bytes 148
  7.2 29.5 %all-gather.4.cloned.1.call-start = ((), (), s32[]{:S(2)}) async-start(), calls=%async_computation | async-start | bytes 2621440 | tf_op jit(solution)/shard_map/all_gather | solution.py:54
  7.9 155.1 %all-gather.6.cloned.1.call-start = ((), (), s32[]{:S(2)}) async-start(), calls=%async_computation.1 | async-start | bytes 7864320 | tf_op jit(solution)/shard_map/all_gather | solution.py:68
  163.0 7.1 %copy-start.11 = (bf16[1,768,4096]{2,1,0:T(8,128)(2,1)S(1)}, bf16[1,768,4096]{2,1,0:T(8,128)(2,1)}, u32[]{:S(2)}) copy-start(bf16[1,768,4096]{2,1,0:T(8,128)(2,1)} %all-gather.6.cloned.1.call-done) | copy-start | bytes 18874372
  170.1 5.7 %copy-start.8 = (bf16[768,128]{0,1:T(8,128)(2,1)S(1)}, bf16[768,128]{0,1:T(8,128)(2,1)}, u32[]{:S(2)}) copy-start(bf16[768,128]{0,1:T(8,128)(2,1)} %all-reduce.1) | copy-start | bytes 589828
  181.9 5.0 %copy-start.9 = (bf16[768,128]{0,1:T(8,128)(2,1)S(1)}, bf16[768,128]{0,1:T(8,128)(2,1)}, u32[]{:S(2)}) copy-start(bf16[768,128]{0,1:T(8,128)(2,1)} %all-reduce.1) | copy-start | bytes 589828
  181.9 5.3 %copy-start.2 = (f32[768,4,64]{2,0,1:T(8,128)S(1)}, f32[768,4,64]{2,0,1:T(8,128)}, u32[]{:S(2)}) copy-start(f32[768,4,64]{2,0,1:T(8,128)} %copy.34) | copy-start | bytes 2359300
  181.9 5.3 %copy-start.6 = (f32[768,64]{1,0:T(8,128)S(1)}, f32[768,64]{1,0:T(8,128)}, u32[]{:S(2)}) copy-start(f32[768,64]{1,0:T(8,128)} %get-tuple-element.8) | copy-start | bytes 589828
  181.9 5.3 %copy-start.7 = (f32[768,64]{1,0:T(8,128)S(1)}, f32[768,64]{1,0:T(8,128)}, u32[]{:S(2)}) copy-start(f32[768,64]{1,0:T(8,128)} %get-tuple-element.9) | copy-start | bytes 589828
  186.9 0.9 copy-start.3
  187.2 5.0 %copy-start.10 = (bf16[768,128]{1,0:T(8,128)(2,1)}, bf16[768,128]{1,0:T(8,128)(2,1)S(1)}, u32[]{:S(2)}) copy-start(bf16[768,128]{1,0:T(8,128)(2,1)S(1)} %fusion.19) | copy-start | bytes 589828
  192.2 6.7 %copy-start.4 = (bf16[768,1,64]{2,0,1:T(8,128)(2,1)S(1)}, bf16[768,1,64]{2,0,1:T(8,128)(2,1)}, u32[]{:S(2)}) copy-start(bf16[768,1,64]{2,0,1:T(8,128)(2,1)} %get-tuple-element.7) | copy-start | bytes 294916
  201.2 0.7 copy-start.5
Sparse Core Ops, SparseCore 0:
  9.6 27.0 all-gather.3
  38.2 124.7 all-gather.5
where the time goes:
time: 209 us
  waiting for transfers between devices  91.8 us (44%)
  blocking collectives  56.4 us (27%)
  matrix products  23.9 us (11%)
  between operations  15.6 us (7%)
  other arithmetic  11.9 us (6%)
  local copies, waits for them, and re-layouts  9.21 us (4%)
    all_gather x1, waiting for transfers between devices, body(): piece = lax.all_gather(own_rows, 'tensor', axis=1, tiled=True)  83.2 us
    psum x1, blocking collectives, body(): down_projected = lax.psum(partial_down, 'tensor').astype(jnp.bfloat16)  39.7 us
    all_gather x1, blocking collectives, body(): lax.all_gather(query_up_factors, 'replica', axis=0, tiled=True)  9.98 us
    all_gather x1, waiting for transfers between devices, body(): lax.all_gather(down_factors, 'replica', axis=0, tiled=True)  7.26 us
    all_gather x1, blocking collectives, body(): lax.all_gather(value_up_factors, 'replica', axis=0, tiled=True)  6.69 us
    dot_general x1, matrix products, body(): q_part = jnp.dot(piece, query_matrix, preferred_element_type=jnp.float32)  5.68 us
    unnamed x28, local copies, waits for them, and re-layouts  5.34 us
    dot_general x1, matrix products, body(): v_part = jnp.dot(piece, value_matrix, preferred_element_type=jnp.float32)  4.97 us
  transfers between devices with their start and end apart: 2, of which 2 were waited for; matrix products, arithmetic and copies ran while one was open for 3% of the time, Pallas kernels for 0%

commit v1 on v0

v1 whole, which is shorter than its diff:
```python
import functools

import jax
import jax.numpy as jnp
import numpy as np
from jax import lax
from jax.experimental import pallas as pl
from jax.experimental.pallas import tpu as pltpu
from jax.sharding import PartitionSpec as P

HEAD_SIZE = 128
PAGE = 64
CHUNKS = 4


def rope_tables(length, width):
    half = width // 2
    exponent = np.float32(2.0) * np.arange(half, dtype=np.float32) / np.float32(width)
    frequency = np.exp(-np.log(np.float32(500000.0)) * exponent).astype(np.float32)
    angles = np.arange(length, dtype=np.float32)[:, None] * frequency[None, :]
    cosine, sine = np.cos(angles), np.sin(angles)
    return (
        np.concatenate([cosine, cosine], axis=1).astype(np.float32),
        np.concatenate([-sine, sine], axis=1).astype(np.float32),
    )


def project_kernel(
    n_t, n_r, x_ref, aid_ref, live_ref, cos_ref, sin_ref, wq_ref, wk_ref, wv_ref, dn_ref, uq_ref, uv_ref,
    out_ref,
    xg, acc, dg, ugq, ugv, part, pr, sh, shg,
    zs, zr, asend, arecv, rs_s, rs_r, ag_s, ag_r,
):
    me = lax.axis_index("tensor")
    rep = lax.axis_index("replica")
    chip, core = rep // 2, rep % 2
    n_x = n_r // 2
    mate = chip * 2 + 1 - core
    T, F = x_ref.shape
    R = T // CHUNKS
    S = T // n_t
    per = dn_ref.shape[0]
    rank = uq_ref.shape[1]
    qw, kw = wq_ref.shape[1], wk_ref.shape[1]

    def tensor_peer(i):
        return lax.rem(me + i, n_t)

    def same_core(i):
        return lax.rem(chip + i, n_x) * 2 + core

    barrier = pltpu.get_barrier_semaphore()
    for i in range(1, n_t):
        pl.semaphore_signal(barrier, inc=1, device_id={"tensor": tensor_peer(i)})
    for i in range(1, n_x):
        pl.semaphore_signal(barrier, inc=1, device_id={"replica": same_core(i)})
    pl.semaphore_signal(barrier, inc=1, device_id={"replica": mate})
    pl.semaphore_wait(barrier, n_t - 1 + n_x - 1 + 1)

    def rows_of(c):
        return pl.ds(pl.multiple_of(c * R, R), R)

    def item(side, d, c):
        sgn = 1 - 2 * side
        ref = xg.at[me - sgn * d, rows_of(c)]
        return pltpu.make_async_remote_copy(
            src_ref=ref, dst_ref=ref, send_sem=zs.at[side, d, c], recv_sem=zr.at[side, d, c],
            device_id={"tensor": me + sgn})

    def arrival(side, d, c):
        sgn = 1 - 2 * side
        ref = xg.at[me - sgn * d, rows_of(c)]
        return pltpu.make_async_remote_copy(
            src_ref=ref, dst_ref=ref, send_sem=zs.at[side, d - 1, c], recv_sem=zr.at[side, d - 1, c],
            device_id={"tensor": me})

    def inside(t):
        return (t >= 0) & (t < n_t)

    def send_own(c, carry):
        xg[me, rows_of(c)] = x_ref[rows_of(c)]
        for side in range(2):
            @pl.when(inside(me + 1 - 2 * side))
            def _():
                item(side, 0, c).start()
        return carry

    lax.fori_loop(0, CHUNKS, send_own, 0)

    pools = ((dn_ref, dg), (uq_ref, ugq), (uv_ref, ugv))

    def pool_copy(k, slot, i, j, to, own):
        src = pools[k][0] if own else pools[k][1].at[slot]
        return pltpu.make_async_remote_copy(
            src_ref=src, dst_ref=pools[k][1].at[slot], send_sem=asend.at[k, i, j],
            recv_sem=arecv.at[k, i, j], device_id={"replica": to})

    for k in range(3):
        for i in range(1, n_x):
            pool_copy(k, rep, i, 0, same_core(i), True).start()
        pool_copy(k, rep, 0, 1, mate, True).start()
        pools[k][1][rep] = pools[k][0][...]

    def mac(src, c, first=False):
        rows = rows_of(c)
        x = xg[src, rows]
        feat = pl.ds(pl.multiple_of(src * F, F), F)
        lo = 0
        for w_ref in (wq_ref, wk_ref, wv_ref):
            width = w_ref.shape[1]
            term = jnp.dot(x, w_ref[feat, :], preferred_element_type=jnp.float32)
            if first:
                acc[rows, lo:lo + width] = term
            else:
                acc[rows, lo:lo + width] += term
            lo += width

    def own_mac(c, carry):
        mac(me, c, True)
        return carry

    lax.fori_loop(0, CHUNKS, own_mac, 0)

    for i in range(1, n_x):
        slot = lax.rem(chip + n_x - i, n_x) * 2 + core
        for k in range(3):
            pool_copy(k, slot, i, 0, mate, False).wait_recv()
            pool_copy(k, slot, i, 1, mate, False).start()
    for i in range(n_x):
        slot = lax.rem(chip + n_x - i, n_x) * 2 + 1 - core
        for k in range(3):
            pool_copy(k, slot, i, 1, mate, False).wait_recv()

    part[...] = jnp.zeros_like(part)

    def down(a, carry):
        term = jnp.dot(x_ref[...], dg[a // per, a % per], preferred_element_type=jnp.float32)
        part[...] += jnp.where(aid_ref[...] == a, term, 0.0)
        return carry

    lax.fori_loop(0, n_r * per, down, 0)

    def rs_copy(t, i):
        return pltpu.make_async_remote_copy(
            src_ref=part.at[pl.ds(pl.multiple_of(t * S, S), S)], dst_ref=pr.at[me],
            send_sem=rs_s.at[i], recv_sem=rs_r.at[i], device_id={"tensor": t})

    def ag_copy(t, i):
        return pltpu.make_async_remote_copy(
            src_ref=sh, dst_ref=shg.at[me], send_sem=ag_s.at[i], recv_sem=ag_r.at[i],
            device_id={"tensor": t})

    for i in range(1, n_t):
        rs_copy(tensor_peer(i), i).start()
    pr[me] = part[pl.ds(pl.multiple_of(me * S, S), S)]

    def phase(first, last):
        def step(k, carry):
            d, c = first + k // CHUNKS, k % CHUNKS

            def one(side, carry):
                sgn = 1 - 2 * side
                src = me - sgn * d

                @pl.when(inside(src))
                def _():
                    arrival(side, d, c).wait_recv()

                    @pl.when(inside(me + sgn))
                    def _():
                        item(side, d, c).start()

                    mac(src, c)

                return carry

            return lax.fori_loop(0, 2, one, carry)

        lax.fori_loop(0, (last - first + 1) * CHUNKS, step, 0)

    phase(1, 1)

    def slot_copy(buf, i, send, recv):
        slot = lax.rem(me + n_t - i, n_t)
        return pltpu.make_async_remote_copy(
            src_ref=buf.at[slot], dst_ref=buf.at[slot], send_sem=send.at[i], recv_sem=recv.at[i],
            device_id={"tensor": me})

    for i in range(1, n_t):
        slot_copy(pr, i, rs_s, rs_r).wait_recv()
    total = pr[0]
    for t in range(1, n_t):
        total = total + pr[t]
    sh[...] = total.astype(jnp.bfloat16)
    for i in range(1, n_t):
        ag_copy(tensor_peer(i), i).start()
    shg[me] = sh[...]

    if n_t > 2:
        phase(2, n_t - 1)

    for i in range(1, n_t):
        slot_copy(shg, i, ag_s, ag_r).wait_recv()

    def finish(t, carry):
        rows = pl.ds(pl.multiple_of(t * S, S), S)
        shrunk = shg[t]
        ids = aid_ref[rows]
        zero = jnp.zeros_like(shrunk)

        def up(a, carry):
            mine = jnp.where(ids == a, shrunk.astype(jnp.float32), 0.0).astype(jnp.bfloat16)
            acc[rows, 0:qw] += jnp.dot(mine[:, :rank], ugq[a // per, a % per], preferred_element_type=jnp.float32)
            acc[rows, qw + kw:] += jnp.dot(mine[:, rank:], ugv[a // per, a % per], preferred_element_type=jnp.float32)
            return carry

        lax.fori_loop(0, n_r * per, up, 0)
        cosine, sine = cos_ref[rows], sin_ref[rows]
        live = live_ref[rows] > 0
        for lo in range(0, qw + 2 * kw, HEAD_SIZE):
            v = acc[rows, lo:lo + HEAD_SIZE]
            if lo < qw + kw:
                v = v * cosine + pltpu.roll(v, HEAD_SIZE // 2, 1) * sine
            if lo >= qw:
                v = jnp.where(live, v, 0.0)
            out_ref[rows, lo:lo + HEAD_SIZE] = v.astype(jnp.bfloat16)
        return carry

    lax.fori_loop(0, n_t, finish, 0)

    def drain(k, carry):
        d, c = k // CHUNKS, k % CHUNKS
        for side in range(2):
            sgn = 1 - 2 * side

            @pl.when(inside(me - sgn * d) & inside(me + sgn))
            def _():
                item(side, d, c).wait_send()
        return carry

    lax.fori_loop(0, (n_t - 1) * CHUNKS, drain, 0)
    for i in range(1, n_t):
        rs_copy(tensor_peer(i), i).wait_send()
        ag_copy(tensor_peer(i), i).wait_send()
    for k in range(3):
        pool_copy(k, rep, 0, 1, mate, True).wait_send()
        for i in range(1, n_x):
            slot = lax.rem(chip + n_x - i, n_x) * 2 + core
            pool_copy(k, rep, i, 0, same_core(i), True).wait_send()
            pool_copy(k, slot, i, 1, mate, False).wait_send()


def attend_kernel(qw, kw, length_ref, page_ref, qkv_ref, out_ref, pages_ref):
    T = qkv_ref.shape[0]
    tile = 256
    group = qw // kw
    length = length_ref[0]
    for p in range(T // PAGE):
        at = page_ref[0, p]
        pages_ref[at, 0] = qkv_ref[p * PAGE:(p + 1) * PAGE, qw:qw + kw]
        pages_ref[at, 1] = qkv_ref[p * PAGE:(p + 1) * PAGE, qw + kw:]
    for i in range(T // tile):
        rows = slice(i * tile, (i + 1) * tile)
        seen = (i + 1) * tile
        t = lax.broadcasted_iota(jnp.int32, (tile, seen), 0) + i * tile
        s = lax.broadcasted_iota(jnp.int32, (tile, seen), 1)
        causal = s <= t
        live = lax.broadcasted_iota(jnp.int32, (tile, HEAD_SIZE), 0) + i * tile < length
        for h in range(qw // HEAD_SIZE):
            g = (h // group) * HEAD_SIZE
            q = qkv_ref[rows, h * HEAD_SIZE:(h + 1) * HEAD_SIZE]
            key = qkv_ref[0:seen, qw + g:qw + g + HEAD_SIZE]
            val = qkv_ref[0:seen, qw + kw + g:qw + kw + g + HEAD_SIZE]
            scores = lax.dot_general(q, key, (((1,), (1,)), ((), ())), preferred_element_type=jnp.float32)
            scores = jnp.where(causal, scores * HEAD_SIZE ** -0.5, -jnp.inf)
            weights = jnp.exp(scores - jnp.max(scores, axis=-1, keepdims=True))
            probs = (weights / jnp.sum(weights, axis=-1, keepdims=True)).astype(jnp.bfloat16)
            mixed = jnp.dot(probs, val, preferred_element_type=jnp.float32)
            out_ref[rows, h * HEAD_SIZE:(h + 1) * HEAD_SIZE] = jnp.where(live, mixed, 0.0).astype(jnp.bfloat16)


def body(n_t, n_r, tokens, lengths, block_adapter_index, cache_page_index, query_matrix, key_matrix, value_matrix,
         down_factors, query_up_factors, value_up_factors):
    T, F = tokens.shape[1:]
    qw, kw = query_matrix.shape[1], key_matrix.shape[1]
    per, rank = query_up_factors.shape[:2]
    bf16, f32 = jnp.bfloat16, jnp.float32
    aid = jnp.broadcast_to(block_adapter_index.reshape(1, 1), (T, 1))
    live = (jnp.arange(T, dtype=jnp.int32)[:, None] < lengths[0]).astype(jnp.int32)
    cosine, sine = rope_tables(T, HEAD_SIZE)
    n_x = n_r // 2
    vmem = pl.BlockSpec(memory_space=pltpu.VMEM)
    smem = pl.BlockSpec(memory_space=pltpu.SMEM)
    dma = pltpu.SemaphoreType.DMA
    qkv = pl.pallas_call(
        functools.partial(project_kernel, n_t, n_r),
        out_shape=jax.ShapeDtypeStruct((T, qw + 2 * kw), bf16),
        in_specs=[vmem] * 11,
        out_specs=vmem,
        scratch_shapes=[
            pltpu.VMEM((n_t, T, F), bf16),
            pltpu.VMEM((T, qw + 2 * kw), f32),
            pltpu.VMEM((n_r,) + down_factors.shape, bf16),
            pltpu.VMEM((n_r,) + query_up_factors.shape, bf16),
            pltpu.VMEM((n_r,) + value_up_factors.shape, bf16),
            pltpu.VMEM((T, 2 * rank), f32),
            pltpu.VMEM((n_t, T // n_t, 2 * rank), f32),
            pltpu.VMEM((T // n_t, 2 * rank), bf16),
            pltpu.VMEM((n_t, T // n_t, 2 * rank), bf16),
            dma((2, n_t - 1, CHUNKS)), dma((2, n_t - 1, CHUNKS)),
            dma((3, n_x, 2)), dma((3, n_x, 2)),
            dma((n_t,)), dma((n_t,)), dma((n_t,)), dma((n_t,)),
        ],
        compiler_params=pltpu.CompilerParams(
            collective_id=0, has_side_effects=True, vmem_limit_bytes=56 * 1024 * 1024),
        name="project",
    )(tokens[0], aid, live, jnp.asarray(cosine), jnp.asarray(sine), query_matrix, key_matrix, value_matrix,
      down_factors, query_up_factors, value_up_factors)
    attended, pages = pl.pallas_call(
        functools.partial(attend_kernel, qw, kw),
        out_shape=(
            jax.ShapeDtypeStruct((T, qw), bf16),
            jax.ShapeDtypeStruct((T // PAGE, 2, PAGE, kw), bf16),
        ),
        in_specs=[smem, smem, vmem],
        out_specs=(vmem, vmem),
        compiler_params=pltpu.CompilerParams(vmem_limit_bytes=48 * 1024 * 1024),
        name="attend",
    )(lengths, cache_page_index, qkv)
    return attended[None], pages[None]


def solution(mesh):
    in_specs = (
        P(("groups", "replica"), None, "tensor"),
        P(("groups", "replica")),
        P(("groups", "replica")),
        P(("groups", "replica"), None),
        P(None, "tensor"),
        P(None, "tensor"),
        P(None, "tensor"),
        P("replica", "tensor", None),
        P("replica", None, "tensor"),
        P("replica", None, "tensor"),
    )
    out_specs = (
        P(("groups", "replica"), None, "tensor"),
        P(("groups", "replica"), None, None, None, "tensor"),
    )
    return jax.shard_map(
        functools.partial(body, mesh.shape["tensor"], mesh.shape["replica"]),
        mesh=mesh, in_specs=in_specs, out_specs=out_specs, check_vma=False)
```

time: 209 us -> 145 us (0.69)
  Pallas kernels: 0 us -> 140 us
  waiting for transfers between devices: 91.8 us -> 0 us
  blocking collectives: 56.4 us -> 0 us
  matrix products: 23.9 us -> 0 us
  between operations: 15.6 us -> 1.95 us
  other arithmetic: 11.9 us -> 0.79 us
  local copies, waits for them, and re-layouts: 9.21 us -> 2.04 us
    pallas_call x0 -> x2, Pallas kernels: none -> 140 us  [the longest x1 134 us: body(): pl.pallas_call(functools.partial(project_kernel, n_t, n_r), out_shape=jax...]
    all_gather x2 -> x0, waiting for transfers between devices: 90.4 us -> none  [the longest x1 83.2 us: body(): piece = lax.all_gather(own_rows, 'tensor', axis=1, tiled=True)]
    psum x1 -> x0, blocking collectives: 39.7 us -> none  [body(): down_projected = lax.psum(partial_down, 'tensor').astype(jnp.bfloat16)]
    dot_general x8 -> x0, matrix products: 23.9 us -> none  [the longest x1 5.68 us: body(): q_part = jnp.dot(piece, query_matrix, preferred_element_type=jnp.float32)]
    all_gather x2 -> x0, blocking collectives: 16.7 us -> none  [the longest x1 9.98 us: body(): lax.all_gather(query_up_factors, 'replica', axis=0, tiled=True)]
    reduce_sum x4 -> x0, other arithmetic: 4.33 us -> none  [the longest x3 2.28 us: body(): jnp.sum(jnp.where(mask, piece, jnp.zeros_like(piece)), axis=0)]
    unnamed x28 -> x4, local copies, waits for them, and re-layouts: 5.34 us -> 1.27 us
    sub x1 -> x0, other arithmetic: 2.37 us -> none  [rotate(): first * cos_rows - second * sin_rows]
  transfers between devices with their start and end apart: 2 -> 0, of which waited for: 2 -> 0; matrix products, arithmetic and copies ran while one was open for 3% -> 0% of each run, Pallas kernels for 0% -> 0%
where the time goes in v1:
time: 145 us
  Pallas kernels  140 us (97%)
  local copies, waits for them, and re-layouts  2.04 us (1%)
  between operations  1.95 us (1%)
    pallas_call x1, Pallas kernels, body(): pl.pallas_call(functools.partial(project_kernel, n_t, n_r), out_shape=jax...  134 us
    pallas_call x1, Pallas kernels, body(): pl.pallas_call(functools.partial(attend_kernel, qw, kw), out_shape=(jax.S...  6.6 us

profile of v1, /device:TPU:0, one launch (start us, length us, event | category | flops | bytes accessed | tf_op | source)
XLA Modules:
  0.0 144.9 jit_solution(14130166093779094208)
XLA Ops:
  1.9 0.8 broadcast_in_dim.15.aid_ref
  2.7 0.8 fusion.live_ref
  3.5 0.0 copy-start.1
  3.5 133.5 %project.1.qkv_ref = bf16[768,768]{1,0:T(8,128)(2,1)} custom-call(bf16[768,1024]{1,0:T(8,128)(2,1)} %bitcast.7, s32[768,1]{1,0:T(8,128)} %broadcast_in_dim.15.aid_ref, s32[768,1]{1,0:T(8,128)} %fusion.live_ref, f32[768,128]{1,0:T(8,128)} %constant.4.clone.cos_ref, f32[768,128]{1,0:T(8,128)} %constant.5.clone.sin_ref, bf16[4096,512]{1,0:T(8,128)(2,1)} %wq_ref.1, ...), custom_call_target="tpu_custom_call" | custom-call | tf_op jit(solution)/shard_map/project/pallas_call | solution.py:295
  137.0 0.0 copy-done.1
  137.0 0.0 copy-start
  137.0 1.3 copy-done
  138.3 6.6 %attend.1 = (bf16[768,512]{1,0:T(8,128)(2,1)}, bf16[12,2,64,128]{3,2,1,0:T(8,128)(2,1)}) custom-call(s32[1]{0:T(128)} %copy.14.length_ref, s32[1,12]{1,0:T(1,128)S(1)} %copy-done.1, bf16[768,768]{1,0:T(8,128)(2,1)S(1)} %copy-done), custom_call_target="tpu_custom_call" | custom-call | tf_op jit(solution)/shard_map/attend/pallas_call | solution.py:319
Async XLA Ops:
  3.5 133.5 %copy-start.1 = (s32[1,12]{1,0:T(1,128)S(1)}, s32[1,12]{1,0:T(1,128)}, u32[]{:S(2)}) copy-start(s32[1,12]{1,0:T(1,128)} %page_ref.1) | copy-start | bytes 148
  137.0 1.3 copy-start

commit v2 on v1

v2 whole, which is shorter than its diff:
```python
import functools

import jax
import jax.numpy as jnp
import numpy as np
from jax import lax
from jax.experimental import pallas as pl
from jax.experimental.pallas import tpu as pltpu
from jax.sharding import PartitionSpec as P

HEAD_SIZE = 128
PAGE = 64
CHUNKS = 4


def rope_tables(length, width):
    half = width // 2
    exponent = np.float32(2.0) * np.arange(half, dtype=np.float32) / np.float32(width)
    frequency = np.exp(-np.log(np.float32(500000.0)) * exponent).astype(np.float32)
    angles = np.arange(length, dtype=np.float32)[:, None] * frequency[None, :]
    cosine, sine = np.cos(angles), np.sin(angles)
    terms = []
    for table in (np.concatenate([cosine, cosine], axis=1), np.concatenate([-sine, sine], axis=1)):
        rest = table.astype(np.float32)
        for _ in range(3):
            term = rest.astype(jnp.bfloat16)
            terms.append(term)
            rest = rest - term.astype(np.float32)
    return np.concatenate(terms, axis=1)


def project_kernel(
    n_t, n_r, x_ref, meta_ref, tab_ref, wq_ref, wk_ref, wv_ref, dn_ref, uq_ref, uv_ref,
    out_ref,
    meta, packed, mb, zb, xb, xg, acc, aid, rope, dg, ugq, ugv, part, pr, sh, shg, qg,
    ms, mr, as_, ar_, bs, br, zs, zr, asend, arecv, rs_s, rs_r, ag_s, ag_r, es, er,
):
    me = lax.axis_index("tensor")
    rep = lax.axis_index("replica")
    chip, core = rep // 2, rep % 2
    n_x = n_r // 2
    mate = chip * 2 + 1 - core
    B, F = x_ref.shape
    T = xg.shape[1]
    R = T // CHUNKS
    S = T // n_t
    per = dn_ref.shape[0]
    rank = uq_ref.shape[1]
    qw, kw = wq_ref.shape[1], wk_ref.shape[1]
    bf16, f32, i32 = jnp.bfloat16, jnp.float32, jnp.int32

    def tensor_peer(i):
        return lax.rem(me + i, n_t)

    def same_core(i):
        return lax.rem(chip + i, n_x) * 2 + core

    def from_chip(i):
        return lax.rem(chip + n_x - i, n_x)

    barrier = pltpu.get_barrier_semaphore()
    for i in range(1, n_t):
        pl.semaphore_signal(barrier, inc=1, device_id={"tensor": tensor_peer(i)})
    for i in range(1, n_r):
        pl.semaphore_signal(barrier, inc=1, device_id={"replica": lax.rem(rep + i, n_r)})
    pl.semaphore_wait(barrier, n_t - 1 + n_r - 1)

    def remote(src, dst, send, recv, **to):
        return pltpu.make_async_remote_copy(
            src_ref=src, dst_ref=dst, send_sem=send, recv_sem=recv, device_id=to)

    def rows_of(c):
        return pl.ds(pl.multiple_of(c * R, R), R)

    def meta_copy(i):
        return remote(meta_ref, meta.at[rep], ms.at[i], mr.at[i], replica=lax.rem(rep + i, n_r))

    for i in range(1, n_r):
        meta_copy(i).start()
    meta[rep] = meta_ref[...]
    for i in range(1, n_r):
        slot = lax.rem(rep + n_r - i, n_r)
        remote(meta.at[slot], meta.at[slot], ms.at[i], mr.at[i], replica=rep).wait_recv()
    own_len = meta_ref[0:1, :]
    offs = []
    total = jnp.zeros_like(own_len)
    own_off = total
    for r in range(n_r):
        offs.append(total)
        own_off = jnp.where(rep == r, total, own_off)
        total = total + meta[r, 0:1, :]

    def send_pack(c, carry):
        width = n_r * R
        g = lax.broadcasted_iota(i32, (width, B), 0)
        t = lax.broadcasted_iota(i32, (width, B), 1)
        owner = lax.rem(g // R, n_x) * 2 + g // (R * n_x)
        place = owner * T + c * R + lax.rem(g, R)
        pick = (place == t + own_off[:, 0:1]) & (t < own_len[:, 0:1])
        rows = jnp.dot(pick.astype(f32).astype(bf16), x_ref[...], preferred_element_type=f32)
        packed[c] = rows.astype(bf16).reshape(2, n_x, R, F)
        mate_copy(c).start()
        return carry

    def mate_copy(c):
        return remote(packed.at[c, 1 - core], mb.at[c], as_.at[c], ar_.at[c], replica=mate)

    def chip_copy(c, i):
        return remote(zb.at[c, lax.rem(chip + i, n_x)], xb.at[c, i], bs.at[c, i], br.at[c, i], replica=same_core(i))

    def send_chip(c, carry):
        mate_copy(c).wait_recv()
        zb[c] = packed[c, core] + mb[c]
        for i in range(1, n_x):
            chip_copy(c, i).start()
        return carry

    def pack_step(c, carry):
        send_pack(c, carry)
        send_chip(c - 1, carry)
        return carry

    send_pack(0, 0)
    lax.fori_loop(1, CHUNKS, pack_step, 0)
    send_chip(CHUNKS - 1, 0)

    pools = ((dn_ref, dg), (uq_ref, ugq), (uv_ref, ugv))

    def pool_copy(k, slot, i, j, to, own):
        src = pools[k][0] if own else pools[k][1].at[slot]
        return remote(src, pools[k][1].at[slot], asend.at[k, i, j], arecv.at[k, i, j], replica=to)

    for k in range(3):
        for i in range(1, n_x):
            pool_copy(k, rep, i, 0, same_core(i), True).start()
        pool_copy(k, rep, 0, 1, mate, True).start()
        pools[k][1][rep] = pools[k][0][...]

    def item(side, d, c):
        sgn = 1 - 2 * side
        ref = xg.at[me - sgn * d, rows_of(c)]
        return remote(ref, ref, zs.at[side, d, c], zr.at[side, d, c], tensor=me + sgn)

    def arrival(side, d, c):
        sgn = 1 - 2 * side
        ref = xg.at[me - sgn * d, rows_of(c)]
        return remote(ref, ref, zs.at[side, d - 1, c], zr.at[side, d - 1, c], tensor=me)

    def inside(t):
        return (t >= 0) & (t < n_t)

    def mac(src, c, first=False):
        rows = rows_of(c)
        x = xg[src, rows]
        feat = pl.ds(pl.multiple_of(src * F, F), F)
        lo = 0
        for w_ref in (wq_ref, wk_ref, wv_ref):
            width = w_ref.shape[1]
            term = jnp.dot(x, w_ref[feat, :], preferred_element_type=f32)
            if first:
                acc[rows, lo:lo + width] = term
            else:
                acc[rows, lo:lo + width] += term
            lo += width

    def send_own(c, carry):
        value = zb[c, chip]
        for i in range(1, n_x):
            chip_copy(c, i).wait_recv()
            value = value + xb[c, i]
        xg[me, rows_of(c)] = value
        for side in range(2):
            @pl.when(inside(me + 1 - 2 * side))
            def _():
                item(side, 0, c).start()
        mac(me, c, True)
        return carry

    lax.fori_loop(0, CHUNKS, send_own, 0)

    place = lax.broadcasted_iota(i32, (T, 128), 0) + rep * T
    ids = jnp.zeros((T, 128), i32)
    pos = jnp.zeros((T, 128), i32)
    for r in range(n_r):
        mine = (place >= offs[r]) & (place < offs[r] + meta[r, 0:1, :])
        ids = jnp.where(mine, meta[r, 1:2, :], ids)
        pos = jnp.where(mine, place - offs[r], pos)
    aid[...] = ids
    pick = lax.broadcasted_iota(i32, (T, B), 1) == pos[:, 0:1]
    found = jnp.dot(pick.astype(f32).astype(bf16), tab_ref[...], preferred_element_type=f32)
    H = HEAD_SIZE
    rope[0] = found[:, 0:H] + found[:, H:2 * H] + found[:, 2 * H:3 * H]
    rope[1] = found[:, 3 * H:4 * H] + found[:, 4 * H:5 * H] + found[:, 5 * H:6 * H]

    def return_copy(slot, c, i, j, to):
        ref = qg.at[slot, rows_of(c)]
        return remote(ref, ref, es.at[c, i, j], er.at[c, i, j], replica=to)

    def finish(c):
        rows = rows_of(c)
        for lo in range(0, qw + 2 * kw, H):
            v = acc[rows, lo:lo + H]
            if lo < qw + kw:
                v = v * rope[0, rows] + pltpu.roll(v, H // 2, 1) * rope[1, rows]
            qg[rep, rows, lo:lo + H] = v.astype(bf16)
        for i in range(1, n_x):
            return_copy(rep, c, i, 0, same_core(i)).start()
        return_copy(rep, c, 0, 1, mate).start()

    def pass_on(c):
        for i in range(1, n_x):
            slot = from_chip(i) * 2 + core
            return_copy(slot, c, i, 0, rep).wait_recv()
            return_copy(slot, c, i, 1, mate).start()

    def phase(first, last, end=False):
        def step(k, carry):
            d, c = k // CHUNKS + 1, lax.rem(k, CHUNKS)

            def one(side, carry):
                sgn = 1 - 2 * side
                src = me - sgn * d

                @pl.when(inside(src))
                def _():
                    arrival(side, d, c).wait_recv()
                    if not end:
                        @pl.when(inside(me + sgn))
                        def _():
                            item(side, d, c).start()

                    mac(src, c)

                return carry

            lax.fori_loop(0, 2, one, 0)
            if end:
                finish(c)

                @pl.when(c > 0)
                def _():
                    pass_on(c - 1)

            return carry

        lax.fori_loop(first, last, step, 0)

    cut = min(CHUNKS + CHUNKS // 2, (n_t - 2) * CHUNKS)
    phase(0, cut)

    for i in range(1, n_x):
        slot = from_chip(i) * 2 + core
        for k in range(3):
            pool_copy(k, slot, i, 0, mate, False).wait_recv()
            pool_copy(k, slot, i, 1, mate, False).start()
    for i in range(n_x):
        slot = from_chip(i) * 2 + 1 - core
        for k in range(3):
            pool_copy(k, slot, i, 1, mate, False).wait_recv()

    part[...] = jnp.zeros_like(part)

    def down(a, carry):
        term = jnp.dot(xg[me], dg[a // per, lax.rem(a, per)], preferred_element_type=f32)
        part[...] += jnp.where(aid[...] == a, term, 0.0)
        return carry

    lax.fori_loop(0, n_r * per, down, 0)

    def share(t):
        return pl.ds(pl.multiple_of(t * S, S), S)

    def rs_copy(i):
        t = tensor_peer(i)
        return remote(part.at[share(t)], pr.at[me], rs_s.at[i], rs_r.at[i], tensor=t)

    def ag_copy(i):
        return remote(sh, shg.at[share(me)], ag_s.at[i], ag_r.at[i], tensor=tensor_peer(i))

    for i in range(1, n_t):
        rs_copy(i).start()
    pr[me] = part[share(me)]

    phase(cut, (n_t - 2) * CHUNKS)

    for i in range(1, n_t):
        ref = pr.at[lax.rem(me + n_t - i, n_t)]
        remote(ref, ref, rs_s.at[i], rs_r.at[i], tensor=me).wait_recv()
    summed = pr[0]
    for t in range(1, n_t):
        summed = summed + pr[t]
    sh[...] = summed.astype(bf16)
    for i in range(1, n_t):
        ag_copy(i).start()
    shg[share(me)] = sh[...]
    for i in range(1, n_t):
        ref = shg.at[share(lax.rem(me + n_t - i, n_t))]
        remote(ref, ref, ag_s.at[i], ag_r.at[i], tensor=me).wait_recv()

    def up(a, carry):
        mine = jnp.where(aid[...] == a, shg[...].astype(f32), 0.0).astype(bf16)
        acc[:, 0:qw] += jnp.dot(mine[:, :rank], ugq[a // per, lax.rem(a, per)], preferred_element_type=f32)
        acc[:, qw + kw:] += jnp.dot(mine[:, rank:], ugv[a // per, lax.rem(a, per)], preferred_element_type=f32)
        return carry

    lax.fori_loop(0, n_r * per, up, 0)

    phase((n_t - 2) * CHUNKS, (n_t - 1) * CHUNKS, True)
    pass_on(CHUNKS - 1)

    for c in range(CHUNKS):
        for i in range(n_x):
            return_copy(from_chip(i) * 2 + 1 - core, c, i, 1, rep).wait_recv()

    tile = 256

    def unpack(k, carry):
        t = lax.broadcasted_iota(i32, (tile, T), 0) + k * tile
        g = lax.broadcasted_iota(i32, (tile, T), 1)
        rows = None
        for r in range(n_r):
            pick = (g + r * T == t + own_off[:, 0:1]) & (t < own_len[:, 0:1])
            term = jnp.dot(pick.astype(f32).astype(bf16), qg[r], preferred_element_type=f32)
            rows = term if rows is None else rows + term
        out_ref[pl.ds(pl.multiple_of(k * tile, tile), tile), :] = rows.astype(bf16)
        return carry

    lax.fori_loop(0, B // tile, unpack, 0)

    def drain(k, carry):
        d, c = k // CHUNKS, lax.rem(k, CHUNKS)
        for side in range(2):
            sgn = 1 - 2 * side

            @pl.when(inside(me - sgn * d) & inside(me + sgn))
            def _():
                item(side, d, c).wait_send()
        return carry

    lax.fori_loop(0, (n_t - 1) * CHUNKS, drain, 0)
    for i in range(1, n_t):
        rs_copy(i).wait_send()
        ag_copy(i).wait_send()
    for i in range(1, n_r):
        meta_copy(i).wait_send()
    for k in range(3):
        pool_copy(k, rep, 0, 1, mate, True).wait_send()
        for i in range(1, n_x):
            pool_copy(k, rep, i, 0, same_core(i), True).wait_send()
            pool_copy(k, from_chip(i) * 2 + core, i, 1, mate, False).wait_send()

    def drain_chunk(c, carry):
        mate_copy(c).wait_send()
        return_copy(rep, c, 0, 1, mate).wait_send()
        for i in range(1, n_x):
            chip_copy(c, i).wait_send()
            return_copy(rep, c, i, 0, same_core(i)).wait_send()
            return_copy(from_chip(i) * 2 + core, c, i, 1, mate).wait_send()
        return carry

    lax.fori_loop(0, CHUNKS, drain_chunk, 0)


def attend_kernel(qw, kw, length_ref, page_ref, qkv_ref, out_ref, pages_ref):
    T = qkv_ref.shape[0]
    tile = 256
    group = qw // kw
    length = length_ref[0]
    for p in range(T // PAGE):
        at = page_ref[0, p]
        pages_ref[at, 0] = qkv_ref[p * PAGE:(p + 1) * PAGE, qw:qw + kw]
        pages_ref[at, 1] = qkv_ref[p * PAGE:(p + 1) * PAGE, qw + kw:]
    for i in range(T // tile):
        rows = slice(i * tile, (i + 1) * tile)
        seen = (i + 1) * tile
        t = lax.broadcasted_iota(jnp.int32, (tile, seen), 0) + i * tile
        s = lax.broadcasted_iota(jnp.int32, (tile, seen), 1)
        causal = s <= t
        live = lax.broadcasted_iota(jnp.int32, (tile, HEAD_SIZE), 0) + i * tile < length
        for h in range(qw // HEAD_SIZE):
            g = (h // group) * HEAD_SIZE
            q = qkv_ref[rows, h * HEAD_SIZE:(h + 1) * HEAD_SIZE]
            key = qkv_ref[0:seen, qw + g:qw + g + HEAD_SIZE]
            val = qkv_ref[0:seen, qw + kw + g:qw + kw + g + HEAD_SIZE]
            scores = lax.dot_general(q, key, (((1,), (1,)), ((), ())), preferred_element_type=jnp.float32)
            scores = jnp.where(causal, scores * HEAD_SIZE ** -0.5, -jnp.inf)
            weights = jnp.exp(scores - jnp.max(scores, axis=-1, keepdims=True))
            probs = (weights / jnp.sum(weights, axis=-1, keepdims=True)).astype(jnp.bfloat16)
            mixed = jnp.dot(probs, val, preferred_element_type=jnp.float32)
            out_ref[rows, h * HEAD_SIZE:(h + 1) * HEAD_SIZE] = jnp.where(live, mixed, 0.0).astype(jnp.bfloat16)


def body(n_t, n_r, tokens, lengths, block_adapter_index, cache_page_index, query_matrix, key_matrix, value_matrix,
         down_factors, query_up_factors, value_up_factors):
    B, F = tokens.shape[1:]
    T = B // 2
    R = T // CHUNKS
    qw, kw = query_matrix.shape[1], key_matrix.shape[1]
    W = qw + 2 * kw
    rank = query_up_factors.shape[1]
    bf16, f32, i32 = jnp.bfloat16, jnp.float32, jnp.int32
    pair = jnp.concatenate([lengths, block_adapter_index, jnp.zeros((6,), i32)])
    meta = jnp.broadcast_to(pair[:, None], (8, 128))
    n_x = n_r // 2
    vmem = pl.BlockSpec(memory_space=pltpu.VMEM)
    smem = pl.BlockSpec(memory_space=pltpu.SMEM)
    dma = pltpu.SemaphoreType.DMA
    qkv = pl.pallas_call(
        functools.partial(project_kernel, n_t, n_r),
        out_shape=jax.ShapeDtypeStruct((B, W), bf16),
        in_specs=[vmem] * 9,
        out_specs=vmem,
        scratch_shapes=[
            pltpu.VMEM((n_r, 8, 128), i32),
            pltpu.VMEM((CHUNKS, 2, n_x, R, F), bf16),
            pltpu.VMEM((CHUNKS, n_x, R, F), bf16),
            pltpu.VMEM((CHUNKS, n_x, R, F), bf16),
            pltpu.VMEM((CHUNKS, n_x, R, F), bf16),
            pltpu.VMEM((n_t, T, F), bf16),
            pltpu.VMEM((T, W), f32),
            pltpu.VMEM((T, 128), i32),
            pltpu.VMEM((2, T, HEAD_SIZE), f32),
            pltpu.VMEM((n_r,) + down_factors.shape, bf16),
            pltpu.VMEM((n_r,) + query_up_factors.shape, bf16),
            pltpu.VMEM((n_r,) + value_up_factors.shape, bf16),
            pltpu.VMEM((T, 2 * rank), f32),
            pltpu.VMEM((n_t, T // n_t, 2 * rank), f32),
            pltpu.VMEM((T // n_t, 2 * rank), bf16),
            pltpu.VMEM((T, 2 * rank), bf16),
            pltpu.VMEM((n_r, T, W), bf16),
            dma((n_r,)), dma((n_r,)),
            dma((CHUNKS,)), dma((CHUNKS,)),
            dma((CHUNKS, n_x)), dma((CHUNKS, n_x)),
            dma((2, n_t - 1, CHUNKS)), dma((2, n_t - 1, CHUNKS)),
            dma((3, n_x, 2)), dma((3, n_x, 2)),
            dma((n_t,)), dma((n_t,)), dma((n_t,)), dma((n_t,)),
            dma((CHUNKS, n_x, 2)), dma((CHUNKS, n_x, 2)),
        ],
        compiler_params=pltpu.CompilerParams(
            collective_id=0, has_side_effects=True, vmem_limit_bytes=58 * 1024 * 1024),
        name="project",
    )(tokens[0], meta, jnp.asarray(rope_tables(B, HEAD_SIZE)), query_matrix, key_matrix, value_matrix,
      down_factors, query_up_factors, value_up_factors)
    attended, pages = pl.pallas_call(
        functools.partial(attend_kernel, qw, kw),
        out_shape=(
            jax.ShapeDtypeStruct((B, qw), bf16),
            jax.ShapeDtypeStruct((B // PAGE, 2, PAGE, kw), bf16),
        ),
        in_specs=[smem, smem, vmem],
        out_specs=(vmem, vmem),
        compiler_params=pltpu.CompilerParams(vmem_limit_bytes=48 * 1024 * 1024),
        name="attend",
    )(lengths, cache_page_index, qkv)
    return attended[None], pages[None]


def solution(mesh):
    in_specs = (
        P(("groups", "replica"), None, "tensor"),
        P(("groups", "replica")),
        P(("groups", "replica")),
        P(("groups", "replica"), None),
        P(None, "tensor"),
        P(None, "tensor"),
        P(None, "tensor"),
        P("replica", "tensor", None),
        P("replica", None, "tensor"),
        P("replica", None, "tensor"),
    )
    out_specs = (
        P(("groups", "replica"), None, "tensor"),
        P(("groups", "replica"), None, None, None, "tensor"),
    )
    return jax.shard_map(
        functools.partial(body, mesh.shape["tensor"], mesh.shape["replica"]),
        mesh=mesh, in_specs=in_specs, out_specs=out_specs, check_vma=False)
```

time: 145 us -> 111 us (0.77)
  Pallas kernels: 140 us -> 105 us
    pallas_call x1, Pallas kernels: 134 us -> 98.9 us  [body(): pl.pallas_call(functools.partial(project_kernel, n_t, n_r), out_shape=jax...]
where the time goes in v2:
time: 111 us; the launch traced here: 109 us
  Pallas kernels  105 us (95%)
  between operations  1.96 us (2%)
  local copies, waits for them, and re-layouts  1.94 us (2%)
    pallas_call x1, Pallas kernels, body(): pl.pallas_call(functools.partial(project_kernel, n_t, n_r), out_shape=jax...  98.9 us
    pallas_call x1, Pallas kernels, body(): pl.pallas_call(functools.partial(attend_kernel, qw, kw), out_shape=(jax.S...  6.6 us

profile of v2, /device:TPU:0, one launch (start us, length us, event | category | flops | bytes accessed | tf_op | source)
XLA Modules:
  0.0 109.5 jit_solution(493051813250747380)
XLA Ops:
  1.9 0.1 pad_add_fusion
  2.0 0.7 broadcast_in_dim.12.meta_ref
  2.7 0.0 copy-start.1
  2.7 98.9 %project.1.qkv_ref = bf16[768,768]{1,0:T(8,128)(2,1)} custom-call(bf16[768,1024]{1,0:T(8,128)(2,1)} %bitcast.3, s32[8,128]{1,0:T(8,128)} %broadcast_in_dim.12.meta_ref, bf16[768,768]{1,0:T(8,128)(2,1)} %constant.4.clone.tab_ref, bf16[4096,512]{1,0:T(8,128)(2,1)} %wq_ref.1, bf16[4096,128]{1,0:T(8,128)(2,1)} %wk_ref.1, bf16[4096,128]{1,0:T(8,128)(2,1)} %wv_ref.1, ...), custom_call_target="tpu_custom_call" | custom-call | tf_op jit(solution)/shard_map/project/pallas_call | solution.py:408
  101.6 0.0 copy-done.1
  101.6 0.0 copy-start
  101.6 1.3 %copy-done = bf16[768,768]{1,0:T(8,128)(2,1)S(1)} copy-done((bf16[768,768]{1,0:T(8,128)(2,1)S(1)}, bf16[768,768]{1,0:T(8,128)(2,1)}, u32[]{:S(2)}) %copy-start) | copy-done | bytes 1179672
  102.9 6.6 %attend.1 = (bf16[768,512]{1,0:T(8,128)(2,1)}, bf16[12,2,64,128]{3,2,1,0:T(8,128)(2,1)}) custom-call(s32[1]{0:T(128)S(6)} %copy.13.length_ref, s32[1,12]{1,0:T(1,128)S(1)} %copy-done.1, bf16[768,768]{1,0:T(8,128)(2,1)S(1)} %copy-done), custom_call_target="tpu_custom_call" | custom-call | tf_op jit(solution)/shard_map/attend/pallas_call | solution.py:444
  (1 shorter events, 0.0 us)
Async XLA Ops:
  2.7 98.9 %copy-start.1 = (s32[1,12]{1,0:T(1,128)S(1)}, s32[1,12]{1,0:T(1,128)}, u32[]{:S(2)}) copy-start(s32[1,12]{1,0:T(1,128)} %page_ref.1) | copy-start | bytes 148
  101.6 1.3 %copy-start = (bf16[768,768]{1,0:T(8,128)(2,1)S(1)}, bf16[768,768]{1,0:T(8,128)(2,1)}, u32[]{:S(2)}) copy-start(bf16[768,768]{1,0:T(8,128)(2,1)} %project.1.qkv_ref) | copy-start | bytes 3538948

commit v3 on v2

--- a/solution.py
+++ b/solution.py
@@ -30,10 +30,11 @@
 
 
 def project_kernel(
-    n_t, n_r, x_ref, meta_ref, tab_ref, wq_ref, wk_ref, wv_ref, dn_ref, uq_ref, uv_ref,
+    n_t, n_r, x_ref, meta_ref, tab_hbm, wq_hbm, wk_hbm, wv_hbm, dn_ref, uq_ref, uv_ref,
     out_ref,
     meta, packed, mb, zb, xb, xg, acc, aid, rope, dg, ugq, ugv, part, pr, sh, shg, qg,
     ms, mr, as_, ar_, bs, br, zs, zr, asend, arecv, rs_s, rs_r, ag_s, ag_r, es, er,
+    tab_ref, wq_ref, wk_ref, wv_ref, ws,
 ):
     me = lax.axis_index("tensor")
     rep = lax.axis_index("replica")
@@ -58,6 +59,14 @@
     def from_chip(i):
         return lax.rem(chip + n_x - i, n_x)
 
+    loads = [
+        pltpu.make_async_copy(src, dst, ws.at[k])
+        for k, (src, dst) in enumerate(
+            ((wq_hbm, wq_ref), (wk_hbm, wk_ref), (wv_hbm, wv_ref), (tab_hbm, tab_ref)))
+    ]
+    for load in loads:
+        load.start()
+
     barrier = pltpu.get_barrier_semaphore()
     for i in range(1, n_t):
         pl.semaphore_signal(barrier, inc=1, device_id={"tensor": tensor_peer(i)})
@@ -176,6 +185,8 @@
         mac(me, c, True)
         return carry
 
+    for load in loads:
+        load.wait()
     lax.fori_loop(0, CHUNKS, send_own, 0)
 
     place = lax.broadcasted_iota(i32, (T, 128), 0) + rep * T
@@ -245,8 +256,7 @@
 
         lax.fori_loop(first, last, step, 0)
 
-    cut = min(CHUNKS + CHUNKS // 2, (n_t - 2) * CHUNKS)
-    phase(0, cut)
+    phase(0, (n_t - 2) * CHUNKS)
 
     for i in range(1, n_x):
         slot = from_chip(i) * 2 + core
@@ -280,8 +290,6 @@
     for i in range(1, n_t):
         rs_copy(i).start()
     pr[me] = part[share(me)]
-
-    phase(cut, (n_t - 2) * CHUNKS)
 
     for i in range(1, n_t):
         ref = pr.at[lax.rem(me + n_t - i, n_t)]
@@ -372,21 +380,26 @@
         pages_ref[at, 1] = qkv_ref[p * PAGE:(p + 1) * PAGE, qw + kw:]
     for i in range(T // tile):
         rows = slice(i * tile, (i + 1) * tile)
-        seen = (i + 1) * tile
-        t = lax.broadcasted_iota(jnp.int32, (tile, seen), 0) + i * tile
-        s = lax.broadcasted_iota(jnp.int32, (tile, seen), 1)
-        causal = s <= t
+        past = i * tile
+        t = lax.broadcasted_iota(jnp.int32, (tile, tile), 0)
+        causal = lax.broadcasted_iota(jnp.int32, (tile, tile), 1) <= t
         live = lax.broadcasted_iota(jnp.int32, (tile, HEAD_SIZE), 0) + i * tile < length
         for h in range(qw // HEAD_SIZE):
             g = (h // group) * HEAD_SIZE
             q = qkv_ref[rows, h * HEAD_SIZE:(h + 1) * HEAD_SIZE]
-            key = qkv_ref[0:seen, qw + g:qw + g + HEAD_SIZE]
-            val = qkv_ref[0:seen, qw + kw + g:qw + kw + g + HEAD_SIZE]
-            scores = lax.dot_general(q, key, (((1,), (1,)), ((), ())), preferred_element_type=jnp.float32)
-            scores = jnp.where(causal, scores * HEAD_SIZE ** -0.5, -jnp.inf)
-            weights = jnp.exp(scores - jnp.max(scores, axis=-1, keepdims=True))
-            probs = (weights / jnp.sum(weights, axis=-1, keepdims=True)).astype(jnp.bfloat16)
-            mixed = jnp.dot(probs, val, preferred_element_type=jnp.float32)
+            pieces = [(past, past + tile, True)] + ([(0, past, False)] if past else [])
+            scores = []
+            for lo, hi, diagonal in pieces:
+                key = qkv_ref[lo:hi, qw + g:qw + g + HEAD_SIZE]
+                piece = lax.dot_general(q, key, (((1,), (1,)), ((), ())), preferred_element_type=jnp.float32)
+                scores.append(jnp.where(causal, piece, -jnp.inf) if diagonal else piece)
+            peak = functools.reduce(jnp.maximum, [jnp.max(p, axis=-1, keepdims=True) for p in scores])
+            weights = [jnp.exp((p - peak) * HEAD_SIZE ** -0.5) for p in scores]
+            inverse = 1.0 / sum(jnp.sum(w, axis=-1, keepdims=True) for w in weights)
+            mixed = jnp.zeros((tile, HEAD_SIZE), jnp.float32)
+            for (lo, hi, _), w in zip(pieces, weights):
+                val = qkv_ref[lo:hi, qw + kw + g:qw + kw + g + HEAD_SIZE]
+                mixed = mixed + jnp.dot((w * inverse).astype(jnp.bfloat16), val, preferred_element_type=jnp.float32)
             out_ref[rows, h * HEAD_SIZE:(h + 1) * HEAD_SIZE] = jnp.where(live, mixed, 0.0).astype(jnp.bfloat16)
 
 
@@ -408,7 +421,7 @@
     qkv = pl.pallas_call(
         functools.partial(project_kernel, n_t, n_r),
         out_shape=jax.ShapeDtypeStruct((B, W), bf16),
-        in_specs=[vmem] * 9,
+        in_specs=[vmem] * 2 + [pl.BlockSpec(memory_space=pl.ANY)] * 4 + [vmem] * 3,
         out_specs=vmem,
         scratch_shapes=[
             pltpu.VMEM((n_r, 8, 128), i32),
@@ -435,6 +448,11 @@
             dma((3, n_x, 2)), dma((3, n_x, 2)),
             dma((n_t,)), dma((n_t,)), dma((n_t,)), dma((n_t,)),
             dma((CHUNKS, n_x, 2)), dma((CHUNKS, n_x, 2)),
+            pltpu.VMEM((B, 6 * HEAD_SIZE), bf16),
+            pltpu.VMEM(query_matrix.shape, bf16),
+            pltpu.VMEM(key_matrix.shape, bf16),
+            pltpu.VMEM(value_matrix.shape, bf16),
+            dma((4,)),
         ],
         compiler_params=pltpu.CompilerParams(
             collective_id=0, has_side_effects=True, vmem_limit_bytes=58 * 1024 * 1024),

time: 111 us -> 110 us (level)
  no operation moved by 1% of the time
where the time goes in v3:
time: 110 us; the launch traced here: 108 us
  Pallas kernels  104 us (95%)
  between operations  1.96 us (2%)
  local copies, waits for them, and re-layouts  1.94 us (2%)
    pallas_call x1, Pallas kernels, body(): pl.pallas_call(functools.partial(project_kernel, n_t, n_r), out_shape=jax...  98.1 us
    pallas_call x1, Pallas kernels, body(): pl.pallas_call(functools.partial(attend_kernel, qw, kw), out_shape=(jax.S...  6.36 us

profile of v3, /device:TPU:0, one launch (start us, length us, event | category | flops | bytes accessed | tf_op | source)
XLA Modules:
  0.0 108.4 jit_solution(916821865147447267)
XLA Ops:
  1.9 0.1 pad_add_fusion
  2.0 0.7 broadcast_in_dim.12.meta_ref
  2.7 0.0 copy-start.1
  2.7 98.1 %project.1.qkv_ref = bf16[768,768]{1,0:T(8,128)(2,1)} custom-call(bf16[768,1024]{1,0:T(8,128)(2,1)} %bitcast.3, s32[8,128]{1,0:T(8,128)} %broadcast_in_dim.12.meta_ref, bf16[768,768]{1,0:T(8,128)(2,1)} %constant.4.clone.tab_hbm, bf16[4096,512]{1,0:T(8,128)(2,1)} %wq_hbm.1, bf16[4096,128]{1,0:T(8,128)(2,1)} %wk_hbm.1, bf16[4096,128]{1,0:T(8,128)(2,1)} %wv_hbm.1, ...), custom_call_target="tpu_custom_call" | custom-call | tf_op jit(solution)/shard_map/project/pallas_call | solution.py:421
  100.8 0.0 copy-done.1
  100.8 0.0 copy-start
  100.8 1.3 %copy-done = bf16[768,768]{1,0:T(8,128)(2,1)S(1)} copy-done((bf16[768,768]{1,0:T(8,128)(2,1)S(1)}, bf16[768,768]{1,0:T(8,128)(2,1)}, u32[]{:S(2)}) %copy-start) | copy-done | bytes 1179672
  102.1 6.4 %attend.1 = (bf16[768,512]{1,0:T(8,128)(2,1)}, bf16[12,2,64,128]{3,2,1,0:T(8,128)(2,1)}) custom-call(s32[1]{0:T(128)S(6)} %copy.13.length_ref, s32[1,12]{1,0:T(1,128)S(1)} %copy-done.1, bf16[768,768]{1,0:T(8,128)(2,1)S(1)} %copy-done), custom_call_target="tpu_custom_call" | custom-call | tf_op jit(solution)/shard_map/attend/pallas_call | solution.py:462
  (1 shorter events, 0.0 us)
Async XLA Ops:
  2.7 98.1 %copy-start.1 = (s32[1,12]{1,0:T(1,128)S(1)}, s32[1,12]{1,0:T(1,128)}, u32[]{:S(2)}) copy-start(s32[1,12]{1,0:T(1,128)} %page_ref.1) | copy-start | bytes 148
  100.8 1.3 %copy-start = (bf16[768,768]{1,0:T(8,128)(2,1)S(1)}, bf16[768,768]{1,0:T(8,128)(2,1)}, u32[]{:S(2)}) copy-start(bf16[768,768]{1,0:T(8,128)(2,1)} %project.1.qkv_ref) | copy-start | bytes 3538948

commit v4 on v3

--- a/solution.py
+++ b/solution.py
@@ -10,7 +10,7 @@
 
 HEAD_SIZE = 128
 PAGE = 64
-CHUNKS = 4
+CHUNKS = 6
 
 
 def rope_tables(length, width):

time: 110 us -> 111 us (level)
  Pallas kernels: 104 us -> 106 us
    pallas_call x1, Pallas kernels: 98.1 us -> 99.7 us  [body(): pl.pallas_call(functools.partial(project_kernel, n_t, n_r), out_shape=jax...]
where the time goes in v4:
time: 111 us; the launch traced here: 110 us
  Pallas kernels  106 us (95%)
  between operations  1.96 us (2%)
  local copies, waits for them, and re-layouts  1.94 us (2%)
    pallas_call x1, Pallas kernels, body(): pl.pallas_call(functools.partial(project_kernel, n_t, n_r), out_shape=jax...  99.7 us
    pallas_call x1, Pallas kernels, body(): pl.pallas_call(functools.partial(attend_kernel, qw, kw), out_shape=(jax.S...  6.36 us

profile of v4, /device:TPU:0, one launch (start us, length us, event | category | flops | bytes accessed | tf_op | source)
XLA Modules:
  0.0 110.1 jit_solution(14606783982739843625)
XLA Ops:
  1.9 0.1 pad_add_fusion
  2.0 0.7 broadcast_in_dim.12.meta_ref
  2.7 0.0 copy-start.1
  2.7 99.7 %project.1.qkv_ref = bf16[768,768]{1,0:T(8,128)(2,1)} custom-call(bf16[768,1024]{1,0:T(8,128)(2,1)} %bitcast.3, s32[8,128]{1,0:T(8,128)} %broadcast_in_dim.12.meta_ref, bf16[768,768]{1,0:T(8,128)(2,1)} %constant.4.clone.tab_hbm, bf16[4096,512]{1,0:T(8,128)(2,1)} %wq_hbm.1, bf16[4096,128]{1,0:T(8,128)(2,1)} %wk_hbm.1, bf16[4096,128]{1,0:T(8,128)(2,1)} %wv_hbm.1, ...), custom_call_target="tpu_custom_call" | custom-call | tf_op jit(solution)/shard_map/project/pallas_call | solution.py:421
  102.4 0.0 copy-done.1
  102.4 0.0 copy-start
  102.5 1.3 %copy-done = bf16[768,768]{1,0:T(8,128)(2,1)S(1)} copy-done((bf16[768,768]{1,0:T(8,128)(2,1)S(1)}, bf16[768,768]{1,0:T(8,128)(2,1)}, u32[]{:S(2)}) %copy-start) | copy-done | bytes 1179672
  103.7 6.4 %attend.1 = (bf16[768,512]{1,0:T(8,128)(2,1)}, bf16[12,2,64,128]{3,2,1,0:T(8,128)(2,1)}) custom-call(s32[1]{0:T(128)S(6)} %copy.13.length_ref, s32[1,12]{1,0:T(1,128)S(1)} %copy-done.1, bf16[768,768]{1,0:T(8,128)(2,1)S(1)} %copy-done), custom_call_target="tpu_custom_call" | custom-call | tf_op jit(solution)/shard_map/attend/pallas_call | solution.py:462
  (1 shorter events, 0.0 us)
Async XLA Ops:
  2.7 99.8 %copy-start.1 = (s32[1,12]{1,0:T(1,128)S(1)}, s32[1,12]{1,0:T(1,128)}, u32[]{:S(2)}) copy-start(s32[1,12]{1,0:T(1,128)} %page_ref.1) | copy-start | bytes 148
  102.4 1.3 %copy-start = (bf16[768,768]{1,0:T(8,128)(2,1)S(1)}, bf16[768,768]{1,0:T(8,128)(2,1)}, u32[]{:S(2)}) copy-start(bf16[768,768]{1,0:T(8,128)(2,1)} %project.1.qkv_ref) | copy-start | bytes 3538948
